TPU v7x, 32 devices: a whole 2x2x4 slice. The times are simulated.
32 devices in a mesh: layer: 4 (over y, x), feat: 8 (over z, core).
Axes of the slice: x: 2, y: 2, z: 4, core: 2. Of those that a mesh axis runs over, the one named last changes fastest.
Arguments:
- source_decoder: bfloat16 [4, 1024, 8192], P('layer', 'feat'), may hold values from -0.0625 to 0.0625
- reader_encoder: bfloat16 [4, 8192, 6144], P('layer', None, 'feat'), may hold values from -6 to 6
- source_acts: bfloat16 [2048, 4096], P('feat', 'layer'), may hold values from 0 to 2
- target_grads: bfloat16 [2048, 24576], P('feat', 'layer'), may hold values from -0.13183594 to 0.13183594
- pair_source: int32 [4, 8, 24], P('layer', 'feat'), may hold values from 0 to 3
- pair_target: int32 [4, 8, 24], P('layer', 'feat'), may hold values from 0 to 5
- pair_count: int32 [4, 8], P('layer', 'feat'), may hold values from 1 to 24, as said below
Outputs:
- edge_table: float32 [4, 8, 24, 128, 128], P('layer', 'feat')
Inputs may be any that keep to these rules, and one draw needn't show every extreme that they name: `pair_count`: slots at and past the count of a reader layer and column are unused; in every draw some reader layer and column uses all 24 slots.
All inputs are finite; a program needn't handle non-finite values.
Results may differ from a plain program's by a relative error of at most 0.0003.
Values may be sent and summed in bfloat16 or wider, within the bound.
A program may use at most 192 MiB of HBM per device.

v0:
```python
import jax
import jax.numpy as jnp
from jax import lax
from jax.sharding import PartitionSpec as P


def local(
    source_decoder, reader_encoder, source_acts, target_grads, pair_source, pair_target, pair_count
):
    source_rows, target_rows = (
        lax.all_to_all(source_acts, "feat", split_axis=1, concat_axis=0, tiled=True),
        lax.all_to_all(target_grads, "feat", split_axis=1, concat_axis=0, tiled=True),
    )
    encoder = reader_encoder[0]
    block_size = source_decoder.shape[1]
    source_slab = source_rows[None]
    sources = pair_source[0, 0]
    targets = pair_target[0, 0]
    slot_count = sources.shape[0]
    live_count = pair_count[0, 0]
    panel_dec, panel_act = (
        lax.all_gather(source_decoder, "layer", axis=0, tiled=True),
        lax.all_gather(source_slab, "layer", axis=0, tiled=True),
    )

    def one_pair(slot_pos, edge_buffer):
        source = sources[slot_pos]
        target = targets[slot_pos]
        decoder_block = lax.dynamic_index_in_dim(panel_dec, source, 0, keepdims=False)
        enc_block = lax.dynamic_slice_in_dim(encoder, target * block_size, block_size, 1)
        virtual = jnp.dot(decoder_block, enc_block, preferred_element_type=jnp.float32)
        act_block = lax.dynamic_index_in_dim(panel_act, source, 0, keepdims=False)
        grad_block = lax.dynamic_slice_in_dim(target_rows, target * block_size, block_size, 1)
        coact = lax.dot_general(
            act_block, grad_block, (((0,), (0,)), ((), ())), preferred_element_type=jnp.float32
        )
        return lax.dynamic_update_index_in_dim(edge_buffer, virtual * coact, slot_pos, 0)

    edge_table = lax.fori_loop(
        0, live_count, one_pair, jnp.zeros((slot_count, block_size, block_size), jnp.float32)
    )
    return edge_table[None, None]


def solution(mesh):
    in_specs = (
        P("layer", "feat", None),
        P("layer", None, "feat"),
        P("feat", "layer"),
        P("feat", "layer"),
        P("layer", "feat", None),
        P("layer", "feat", None),
        P("layer", "feat"),
    )
    out_specs = P("layer", "feat", None, None, None)
    return jax.shard_map(local, mesh=mesh, in_specs=in_specs, out_specs=out_specs, check_vma=False)
```

profile of v0, /device:TPU:5, one launch (start us, length us, event | category | flops | bytes accessed | tf_op | source)
XLA Modules:
  0.0 375.2 jit_solution(6197434539734011829)
XLA Ops:
  6.5 1.0 copy-done
  7.7 19.8 %all_to_all.35 = bf16[256,8,128]{2,0,1:T(8,128)(2,1)} all-to-all(bf16[256,8,128]{2,0,1:T(8,128)(2,1)S(1)} %copy_bitcast_fusion.1), channel_id=1, replica_groups=mesh['layer'=4,'feat'=8] {'feat'}, dimensions={1} | all-to-all | bytes 1048576 | tf_op jit(solution)/shard_map/all_to_all | solution.py:11
  27.5 0.7 all-gather.3.cloned.1.call-update
  28.2 3.8 %copy.16 = bf16[32,8,8,768]{3,2,0,1:T(8,128)(2,1)} copy(bf16[32,8,8,768]{3,2,1,0:T(8,128)(2,1)} %bitcast.44) | data formatting | bytes 6291456 | tf_op jit(solution)/shard_map/all_to_all | solution.py:12
  32.1 5.5 %all-to-all-start.1 = ((bf16[256,8,768]{2,0,1:T(8,128)(2,1)}), bf16[256,8,768]{2,0,1:T(8,128)(2,1)}, u32[]{:S(2)}, u32[]{:S(2)}) async-start(bf16[256,8,768]{2,0,1:T(8,128)(2,1)} %bitcast.42), calls=%async_computation.1 | async-start | bytes 6291456 | tf_op jit(solution)/shard_map/all_to_all | solution.py:12
  37.6 24.6 %all-gather.5.cloned.1.call-done = bf16[4,2048,128]{2,1,0:T(8,128)(2,1)} async-done(((bf16[1,2048,128]{2,1,0:T(8,128)(2,1)}), bf16[4,2048,128]{2,1,0:T(8,128)(2,1)}) %all-gather.5.cloned.1.call-update) | async-done | bytes 2097168 | tf_op jit(solution)/shard_map/all_gather | solution.py:23
  62.2 46.2 %all-to-all-done.1 = bf16[256,8,768]{2,0,1:T(8,128)(2,1)} async-done(((bf16[256,8,768]{2,0,1:T(8,128)(2,1)}), bf16[256,8,768]{2,0,1:T(8,128)(2,1)}, u32[]{:S(2)}, u32[]{:S(2)}) %all-to-all-start.1) | async-done | bytes 3145760 | tf_op jit(solution)/shard_map/all_to_all | solution.py:12
  108.4 43.3 %all-gather.3.cloned.1.call-done = bf16[4,128,8192]{2,1,0:T(8,128)(2,1)} async-done(((bf16[1,128,8192]{2,1,0:T(8,128)(2,1)}), bf16[4,128,8192]{2,1,0:T(8,128)(2,1)}) %all-gather.3.cloned.1.call-update) | async-done | bytes 8388624 | tf_op jit(solution)/shard_map/all_gather | solution.py:22
  151.8 215.3 %while.10 = (s32[]{:T(128)}, f32[24,128,128]{2,1,0:T(8,128)S(1)}, s32[]{:T(128)}, s32[24]{0:T(128)S(1)}, bf16[4,128,8192]{2,1,0:T(8,128)(2,1)}, /*index=5*/s32[2...) while((s32[]{:T(128)}, f32[24,128,128]{2,1,0:T(8,128)S(1)}, ...), condition=%wide.region_1.2_spmd, body=%wide.region_0.1_spmd.sunk | while | flops 335560704 | bytes 5439787 | solution.py:39
  155.0 0.7 dynamic_slice.42
  156.3 2.9 fusion.22
  159.2 1.5 fusion.23
  164.0 0.7 dynamic_slice.42
  165.2 2.9 fusion.22
  168.2 1.6 fusion.23
  173.0 0.7 dynamic_slice.42
  174.2 2.9 fusion.22
  177.2 1.5 fusion.23
  181.9 0.7 dynamic_slice.42
  183.2 2.9 fusion.22
  186.1 1.5 fusion.23
  190.8 0.7 dynamic_slice.42
  192.1 2.9 fusion.22
  195.0 1.5 fusion.23
  199.8 0.7 dynamic_slice.42
  201.1 2.9 fusion.22
  204.0 1.5 fusion.23
  210.0 2.9 fusion.22
  212.9 1.5 fusion.23
  218.9 2.9 fusion.22
  221.9 1.5 fusion.23
  227.9 2.9 fusion.22
  230.8 1.5 fusion.23
  236.8 2.9 fusion.22
  239.8 1.5 fusion.23
  245.8 2.9 fusion.22
  248.7 1.5 fusion.23
  254.7 2.9 fusion.22
  257.7 1.5 fusion.23
  263.7 2.9 fusion.22
  266.6 1.5 fusion.23
  272.6 2.9 fusion.22
  275.5 1.5 fusion.23
  281.6 2.9 fusion.22
  284.5 1.5 fusion.23
  290.5 2.9 fusion.22
  293.4 1.5 fusion.23
  299.4 2.9 fusion.22
  302.4 1.5 fusion.23
  308.4 2.9 fusion.22
  311.3 1.5 fusion.23
  317.3 2.9 fusion.22
  320.3 1.5 fusion.23
  326.3 2.9 fusion.22
  329.2 1.5 fusion.23
  335.2 2.9 fusion.22
  338.1 1.5 fusion.23
  344.2 2.9 fusion.22
  347.1 1.5 fusion.23
  353.1 2.9 fusion.22
  356.0 1.5 fusion.23
  362.0 2.9 fusion.22
  365.0 1.5 fusion.23
  367.2 1.1 copy-done.1
  (53 shorter events, 27.6 us)
Async XLA Ops:
  6.5 1.0 copy-start
  6.5 55.6 %all-gather.5.cloned.1.call-start = ((), (), s32[]{:S(2)}) async-start(), calls=%async_computation.3 | async-start | bytes 2621440 | tf_op jit(solution)/shard_map/all_gather | solution.py:23
  27.5 124.2 %all-gather.3.cloned.1.call-start = ((), (), s32[]{:S(2)}) async-start(), calls=%async_computation.2 | async-start | bytes 10485760 | tf_op jit(solution)/shard_map/all_gather | solution.py:22
  32.0 119.8 %copy-start.2 = (s32[1,1,24]{2,1,0:T(1,128)S(1)}, s32[1,1,24]{2,1,0:T(1,128)}, u32[]{:S(2)}) copy-start(s32[1,1,24]{2,1,0:T(1,128)} %param.13) | copy-start | bytes 292
  32.1 119.8 %copy-start.3 = (s32[1,1,24]{2,1,0:T(1,128)S(1)}, s32[1,1,24]{2,1,0:T(1,128)}, u32[]{:S(2)}) copy-start(s32[1,1,24]{2,1,0:T(1,128)} %param.14) | copy-start | bytes 292
  32.1 76.3 %all-to-all-start.1 = ((bf16[256,8,768]{2,0,1:T(8,128)(2,1)}), bf16[256,8,768]{2,0,1:T(8,128)(2,1)}, u32[]{:S(2)}, u32[]{:S(2)}) async-start(bf16[256,8,768]{2,0,1:T(8,128)(2,1)} %bitcast.42), calls=%async_computation.1 | async-start | bytes 6291456 | tf_op jit(solution)/shard_map/all_to_all | solution.py:12
  367.2 1.1 copy-start.1
Sparse Core Ops, SparseCore 0:
  27.6 34.5 all-gather.4
  64.0 87.5 all-gather.2
where the time goes:
time: 377 us; the launch traced here: 375 us
  waiting for transfers between devices  115 us (31%)
  matrix products  107 us (28%)
  loops' own time  76.8 us (20%)
  local copies, waits for them, and re-layouts  37.4 us (10%)
  blocking collectives  19.8 us (5%)
  between operations  13.5 us (4%)
  starting transfers between devices  5.58 us (1%)
    another operation x1, loops' own time, local(): lax.fori_loop(0, live_count, one_pair, jnp.zeros((slot_count, block_size,...  76.8 us
    dot_general x24, matrix products, one_pair(): jnp.dot(decoder_block, enc_block, preferred_element_type=jnp.float32)  70.2 us
    all_to_all x1, waiting for transfers between devices, local(): lax.all_to_all(target_grads, 'feat', split_axis=1, concat_axis=0, tiled=T...  46.2 us
    all_gather x1, waiting for transfers between devices, local(): lax.all_gather(source_decoder, 'layer', axis=0, tiled=True)  43.3 us
    dot_general x24, matrix products, one_pair(): lax.dot_general(act_block, grad_block, (((0,), (0,)), ((), ())), preferre...  37.2 us
    all_gather x1, waiting for transfers between devices, local(): lax.all_gather(source_slab, 'layer', axis=0, tiled=True)  24.6 us
    all_to_all x1, blocking collectives, local(): lax.all_to_all(source_acts, 'feat', split_axis=1, concat_axis=0, tiled=True)  19.8 us
    dynamic_slice x24, local copies, waits for them, and re-layouts, one_pair(): target = targets[slot_pos]  15.6 us
  transfers between devices with their start and end apart: 3, of which 3 were waited for; matrix products, arithmetic and copies ran while one was open for 1% of the time, Pallas kernels for 0%

commit v1 on v0

--- a/solution.py
+++ b/solution.py
@@ -2,6 +2,22 @@
 import jax.numpy as jnp
 from jax import lax
 from jax.sharding import PartitionSpec as P
+
+
+def collect(x, axis, dim):
+    ways, here, step = (lax.axis_size(axis), lax.axis_index(axis), x.shape[dim])
+    lengths = [n * ways if d == dim else n for d, n in enumerate(x.shape)]
+    full = lax.dynamic_update_slice_in_dim(jnp.zeros(lengths, x.dtype), x, here * step, axis=dim)
+    going_up = going_down = x
+    for far in range(1, ways // 2 + 1):
+        going_up = lax.ppermute(going_up, axis, [(d, (d + 1) % ways) for d in range(ways)])
+        full = lax.dynamic_update_slice_in_dim(full, going_up, (here - far) % ways * step, axis=dim)
+        if 2 * far < ways:
+            going_down = lax.ppermute(going_down, axis, [(d, (d - 1) % ways) for d in range(ways)])
+            full = lax.dynamic_update_slice_in_dim(
+                full, going_down, (here + far) % ways * step, axis=dim
+            )
+    return full
 
 
 def local(
@@ -19,7 +35,7 @@
     slot_count = sources.shape[0]
     live_count = pair_count[0, 0]
     panel_dec, panel_act = (
-        lax.all_gather(source_decoder, "layer", axis=0, tiled=True),
+        collect(source_decoder, "layer", 0),
         lax.all_gather(source_slab, "layer", axis=0, tiled=True),
     )
 

time: 377 us -> 398 us (1.056)
  blocking collectives: 19.8 us -> 0 us
  waiting for transfers between devices: 115 us -> 131 us
  local copies, waits for them, and re-layouts: 37.4 us -> 51.1 us
  starting transfers between devices: 5.58 us -> 13.5 us
    ppermute x0 -> x3, waiting for transfers between devices: none -> 121 us  [the longest x2 75.2 us: collect(): lax.ppermute(going_up, axis, [(d, (d + 1) % ways) for d in range(ways)])]
    all_to_all x1, waiting for transfers between devices: 46.2 us -> 0.01 us  [local(): lax.all_to_all(target_grads, 'feat', split_axis=1, concat_axis=0, tiled=T...]
    all_gather x1 -> x0, waiting for transfers between devices: 43.3 us -> none  [local(): lax.all_gather(source_decoder, 'layer', axis=0, tiled=True)]
    all_gather x1, waiting for transfers between devices: 24.6 us -> 0.01 us  [local(): lax.all_gather(source_slab, 'layer', axis=0, tiled=True)]
    all_to_all x1 -> x0, blocking collectives: 19.8 us -> none  [local(): lax.all_to_all(source_acts, 'feat', split_axis=1, concat_axis=0, tiled=True)]
    dynamic_update_slice x0 -> x4, local copies, waits for them, and re-layouts: none -> 10.8 us  [the longest x2 6.21 us: collect(): lax.dynamic_update_slice_in_dim(full, going_up, (here - far) % ways * ste...]
    all_to_all x0 -> x1, waiting for transfers between devices: none -> 9.55 us  [local(): lax.all_to_all(source_acts, 'feat', split_axis=1, concat_axis=0, tiled=True)]
    all_to_all x0 -> x1, starting transfers between devices: none -> 5.55 us  [local(): lax.all_to_all(source_acts, 'feat', split_axis=1, concat_axis=0, tiled=True)]
  transfers between devices with their start and end apart: 3 -> 6, of which waited for: 3 -> 4; matrix products, arithmetic and copies ran while one was open for 1% -> 5% of each run, Pallas kernels for 0% -> 0%
where the time goes in v1:
time: 398 us; the launch traced here: 395 us
  waiting for transfers between devices  131 us (33%)
  matrix products  107 us (27%)
  loops' own time  79.4 us (20%)
  local copies, waits for them, and re-layouts  51.1 us (13%)
  starting transfers between devices  13.5 us (3%)
  between operations  13.4 us (3%)
    another operation x1, loops' own time, local(): lax.fori_loop(0, live_count, one_pair, jnp.zeros((slot_count, block_size,...  79.4 us
    ppermute x2, waiting for transfers between devices, collect(): lax.ppermute(going_up, axis, [(d, (d + 1) % ways) for d in range(ways)])  75.2 us
    dot_general x24, matrix products, one_pair(): jnp.dot(decoder_block, enc_block, preferred_element_type=jnp.float32)  70.2 us
    ppermute x1, waiting for transfers between devices, collect(): lax.ppermute(going_down, axis, [(d, (d - 1) % ways) for d in range(ways)])  45.8 us
    dot_general x24, matrix products, one_pair(): lax.dot_general(act_block, grad_block, (((0,), (0,)), ((), ())), preferre...  37.1 us
    dynamic_slice x24, local copies, waits for them, and re-layouts, one_pair(): target = targets[slot_pos]  14.1 us
    dynamic_slice x24, local copies, waits for them, and re-layouts, one_pair(): source = sources[slot_pos]  14.1 us
    all_to_all x1, waiting for transfers between devices, local(): lax.all_to_all(source_acts, 'feat', split_axis=1, concat_axis=0, tiled=True)  9.55 us
  transfers between devices with their start and end apart: 6, of which 4 were waited for; matrix products, arithmetic and copies ran while one was open for 5% of the time, Pallas kernels for 0%

profile of v1, /device:TPU:5, one launch (start us, length us, event | category | flops | bytes accessed | tf_op | source)
XLA Modules:
  0.0 395.4 jit_solution(883295884212652990)
XLA Ops:
  8.5 5.5 %all-to-all-start = ((bf16[256,8,128]{2,0,1:T(8,128)(2,1)}), bf16[256,8,128]{2,0,1:T(8,128)(2,1)S(1)}, u32[]{:S(2)}, u32[]{:S(2)}) async-start(bf16[256,8,128]{2,0,1:T(8,128)(2,1)} %copy_bitcast_fusion.1), calls=%async_computation | async-start | bytes 1048576 | tf_op jit(solution)/shard_map/all_to_all | solution.py:27
  14.0 1.2 collective-permute-start
  15.2 3.8 copy.16
  19.1 9.6 %all-to-all-done = bf16[256,8,128]{2,0,1:T(8,128)(2,1)S(1)} async-done(((bf16[256,8,128]{2,0,1:T(8,128)(2,1)}), bf16[256,8,128]{2,0,1:T(8,128)(2,1)S(1)}, u32[]{:S(2)}, u32[]{:S(2)}) %all-to-all-start) | async-done | bytes 524320 | tf_op jit(solution)/shard_map/all_to_all | solution.py:27
  29.4 5.2 %all-to-all-start.1 = ((bf16[256,8,768]{2,0,1:T(8,128)(2,1)}), bf16[256,8,768]{2,0,1:T(8,128)(2,1)}, u32[]{:S(2)}, u32[]{:S(2)}) async-start(bf16[256,8,768]{2,0,1:T(8,128)(2,1)} %bitcast.42), calls=%async_computation.1 | async-start | bytes 6291456 | tf_op jit(solution)/shard_map/all_to_all | solution.py:28
  34.6 1.2 collective-permute-start.1
  35.9 32.5 %collective-permute-done = bf16[1,128,8192]{2,1,0:T(8,128)(2,1)} collective-permute-done((bf16[1,128,8192]{2,1,0:T(8,128)(2,1)}, bf16[1,128,8192]{2,1,0:T(8,128)(2,1)}, u32[]{:S(2)}, u32[]{:S(2)}) %collective-permute-start) | collective-permute-done | bytes 2097184 | tf_op jit(solution)/shard_map/ppermute | solution.py:13
  68.7 4.2 %broadcast_in_dim.17 = bf16[4,128,8192]{2,1,0:T(8,128)(2,1)} broadcast(bf16[]{:T(256)} %constant.55.clone.1), dimensions={} | broadcast | bytes 8388610 | tf_op jit(solution)/shard_map/broadcast_in_dim | solution.py:10
  72.9 1.5 constant_dynamic-update-slice_fusion.3
  74.4 3.1 constant_dynamic-update-slice_fusion.2
  77.5 45.8 %collective-permute-done.1 = bf16[1,128,8192]{2,1,0:T(8,128)(2,1)} collective-permute-done((bf16[1,128,8192]{2,1,0:T(8,128)(2,1)S(1)}, bf16[1,128,8192]{2,1,0:T(8,128)(2,1)}, u32[]{:S(2)}, u32[]{:S(2)}) %collective-permute-start.1) | collective-permute-done | bytes 2097184 | tf_op jit(solution)/shard_map/ppermute | solution.py:16
  123.3 3.1 constant_dynamic-update-slice_fusion.1
  126.5 42.8 %collective-permute-done.2 = bf16[1,128,8192]{2,1,0:T(8,128)(2,1)} collective-permute-done((bf16[1,128,8192]{2,1,0:T(8,128)(2,1)}, bf16[1,128,8192]{2,1,0:T(8,128)(2,1)}, u32[]{:S(2)}, u32[]{:S(2)}) %collective-permute-start.2) | collective-permute-done | bytes 2097184 | tf_op jit(solution)/shard_map/ppermute | solution.py:13
  169.2 3.1 constant_dynamic-update-slice_fusion
  172.5 214.9 %while.10 = (s32[]{:T(128)}, f32[24,128,128]{2,1,0:T(8,128)S(1)}, s32[]{:T(128)}, s32[24]{0:T(128)S(1)}, bf16[4,128,8192]{2,1,0:T(8,128)(2,1)}, /*index=5*/s32[2...) while((s32[]{:T(128)}, f32[24,128,128]{2,1,0:T(8,128)S(1)}, ...), condition=%wide.region_1.2_spmd, body=%wide.region_0.1_spmd.sunk | while | flops 335560704 | bytes 5439787 | solution.py:55
  177.0 2.9 fusion.22
  179.9 1.5 fusion.23
  185.9 2.9 fusion.22
  188.8 1.5 fusion.23
  194.8 2.9 fusion.22
  197.8 1.5 fusion.23
  203.8 2.9 fusion.22
  206.7 1.5 fusion.23
  212.7 2.9 fusion.22
  215.6 1.5 fusion.23
  221.6 2.9 fusion.22
  224.5 1.5 fusion.23
  230.5 2.9 fusion.22
  233.5 1.5 fusion.23
  239.5 2.9 fusion.22
  242.4 1.5 fusion.23
  248.4 2.9 fusion.22
  251.3 1.5 fusion.23
  257.3 2.9 fusion.22
  260.2 1.5 fusion.23
  266.2 2.9 fusion.22
  269.2 1.5 fusion.23
  275.2 2.9 fusion.22
  278.1 1.5 fusion.23
  284.1 2.9 fusion.22
  287.0 1.5 fusion.23
  293.0 2.9 fusion.22
  295.9 1.5 fusion.23
  301.9 2.9 fusion.22
  304.9 1.5 fusion.23
  310.9 2.9 fusion.22
  313.8 1.5 fusion.23
  319.8 2.9 fusion.22
  322.7 1.5 fusion.23
  328.7 2.9 fusion.22
  331.7 1.5 fusion.23
  337.6 2.9 fusion.22
  340.6 1.5 fusion.23
  346.6 2.9 fusion.22
  349.5 1.5 fusion.23
  355.5 2.9 fusion.22
  358.4 1.5 fusion.23
  364.4 2.9 fusion.22
  367.4 1.5 fusion.23
  373.4 2.9 fusion.22
  376.3 1.5 fusion.23
  382.3 2.9 fusion.22
  385.2 1.5 fusion.23
  387.4 1.1 copy-done.3
  (66 shorter events, 31.4 us)
Async XLA Ops:
  6.5 1.0 copy-start
  8.5 20.1 %all-to-all-start = ((bf16[256,8,128]{2,0,1:T(8,128)(2,1)}), bf16[256,8,128]{2,0,1:T(8,128)(2,1)S(1)}, u32[]{:S(2)}, u32[]{:S(2)}) async-start(bf16[256,8,128]{2,0,1:T(8,128)(2,1)} %copy_bitcast_fusion.1), calls=%async_computation | async-start | bytes 1048576 | tf_op jit(solution)/shard_map/all_to_all | solution.py:27
  14.0 54.3 %collective-permute-start = (bf16[1,128,8192]{2,1,0:T(8,128)(2,1)}, bf16[1,128,8192]{2,1,0:T(8,128)(2,1)}, u32[]{:S(2)}, u32[]{:S(2)}) collective-permute-start(bf16[1,128,8192]{2,1,0:T(8,128)(2,1)} %param.9), channel_id=1, source_target_pairs={{0,8},{8,16},{16,24},{24,0},{1,9},{9,17},{17,25},{25,1},{2,10},{10... | collective-permute-start | bytes 6291464 | tf_op jit(solution)/shard_map/ppermute | solution.py:13
  28.6 0.8 copy-start.2
  28.6 6.0 %copy-start.1 = (bf16[1,128,8192]{2,1,0:T(8,128)(2,1)S(1)}, bf16[1,128,8192]{2,1,0:T(8,128)(2,1)}, u32[]{:S(2)}) copy-start(bf16[1,128,8192]{2,1,0:T(8,128)(2,1)} %param.9) | copy-start | bytes 6291460
  29.4 142.9 %all-to-all-start.1 = ((bf16[256,8,768]{2,0,1:T(8,128)(2,1)}), bf16[256,8,768]{2,0,1:T(8,128)(2,1)}, u32[]{:S(2)}, u32[]{:S(2)}) async-start(bf16[256,8,768]{2,0,1:T(8,128)(2,1)} %bitcast.42), calls=%async_computation.1 | async-start | bytes 6291456 | tf_op jit(solution)/shard_map/all_to_all | solution.py:28
  34.6 137.7 %all-gather.2.cloned.1.call-start = ((), (), s32[]{:S(2)}) async-start(), calls=%async_computation.2 | async-start | bytes 2621440 | tf_op jit(solution)/shard_map/all_gather | solution.py:39
  34.6 88.7 %collective-permute-start.1 = (bf16[1,128,8192]{2,1,0:T(8,128)(2,1)S(1)}, bf16[1,128,8192]{2,1,0:T(8,128)(2,1)}, u32[]{:S(2)}, u32[]{:S(2)}) collective-permute-start(bf16[1,128,8192]{2,1,0:T(8,128)(2,1)S(1)} %copy-done.1), channel_id=1, source_target_pairs={{0,24},{8,0},{16,8},{24,16},{1,25},{9,1},{17,9},{25,17},{2,26},{10... | collective-permute-start | bytes 6291464 | tf_op jit(solution)/shard_map/ppermute | solution.py:16
  68.4 100.9 %collective-permute-start.2 = (bf16[1,128,8192]{2,1,0:T(8,128)(2,1)}, bf16[1,128,8192]{2,1,0:T(8,128)(2,1)}, u32[]{:S(2)}, u32[]{:S(2)}) collective-permute-start(bf16[1,128,8192]{2,1,0:T(8,128)(2,1)} %collective-permute-done), channel_id=1, source_target_pairs={{0,8},{8,16},{16,24},{24,0},{1,9},{9,17},{17,25},{25,1},{2,10},{10... | collective-permute-start | bytes 6291464 | tf_op jit(solution)/shard_map/ppermute | solution.py:13
  126.5 46.0 %copy-start.4 = (s32[1,1,24]{2,1,0:T(1,128)S(1)}, s32[1,1,24]{2,1,0:T(1,128)}, u32[]{:S(2)}) copy-start(s32[1,1,24]{2,1,0:T(1,128)} %param.13) | copy-start | bytes 292
  126.5 46.1 %copy-start.5 = (s32[1,1,24]{2,1,0:T(1,128)S(1)}, s32[1,1,24]{2,1,0:T(1,128)}, u32[]{:S(2)}) copy-start(s32[1,1,24]{2,1,0:T(1,128)} %param.14) | copy-start | bytes 292
  387.4 1.1 copy-start.3
Sparse Core Ops, SparseCore 0:
  37.3 53.1 all-gather.1
